TPU v7x, 32 devices: a whole 2x2x4 slice. The times are simulated.
32 devices in a mesh: tm: 16 (over z, x, core), band: 2 (over y).
Axes of the slice: x: 2, y: 2, z: 4, core: 2. Of those that a mesh axis runs over, the one named last changes fastest.
Arguments:
- query_input: bfloat16 [16, 10, 26, 1120], P('tm', 'band'), may hold values from -6 to 6
- key_input: bfloat16 [16, 10, 26, 1120], P('tm', 'band'), may hold values from -8 to 8
- value_input: bfloat16 [16, 10, 26, 1120], P('tm', 'band'), may hold values from -12 to 12
- cotangent: bfloat16 [16, 10, 26, 1120], P('tm', 'band'), may hold values from -6 to 6
- local_kernel_weight: float32 [3, 3, 1120], replicated, may hold values from -2 to 2
Outputs:
- mixed_out: bfloat16 [16, 10, 26, 1120], P('tm', 'band')
- query_grad: bfloat16 [16, 10, 26, 1120], P('tm', 'band')
- key_grad: bfloat16 [16, 10, 26, 1120], P('tm', 'band')
- value_grad: bfloat16 [16, 10, 26, 1120], P('tm', 'band')
- kernel_grad: float32 [3, 3, 1120], replicated
All inputs are finite; a program needn't handle non-finite values.
Results may differ from a plain program's by a relative error of at most 0.018.
Values may be sent and summed in bfloat16 or wider, within the bound.
A program may use at most 128 MiB of HBM per device.

v0:
```python
import functools
import math

import jax
import jax.numpy as jnp
from jax import lax
from jax.experimental import pallas as pl
from jax.experimental.pallas import tpu as pltpu
from jax.sharding import PartitionSpec as P

HEAD_DIM = 32
LANES = 128
COLS = 32
MESH = pl.DeviceIdType.MESH
F32 = jnp.float32
BF16 = jnp.bfloat16


def groups(wide):
    out, at = [], 0
    while at < wide:
        size = min(256, wide - at)
        out.append((at, size))
        at += size
    return out


def feature(x):
    return jnp.where(x > 0, x + 1.0, jnp.exp(jnp.minimum(x, 0.0)))


def slope(x):
    return jnp.where(x > 0, 1.0, jnp.exp(jnp.minimum(x, 0.0)))


def parts_of(x):
    high = x.astype(BF16)
    return high, (x - high.astype(F32)).astype(BF16)


def mm(a, b):
    return lax.dot_general(a, b, (((1,), (0,)), ((), ())), preferred_element_type=F32)


def mm_bt(a, b):
    return lax.dot_general(a, b, (((1,), (1,)), ((), ())), preferred_element_type=F32)


def mm_at(a, b):
    return lax.dot_general(a, b, (((0,), (0,)), ((), ())), preferred_element_type=F32)


def same_head(size):
    row = lax.broadcasted_iota(jnp.int32, (size, size), 0) // HEAD_DIM
    lane = lax.broadcasted_iota(jnp.int32, (size, size), 1) // HEAD_DIM
    return row == lane


def compress(full, mask):
    size = full.shape[0]
    kept = jnp.where(mask, full, 0.0)
    total = kept[0:HEAD_DIM]
    for h in range(1, size // HEAD_DIM):
        total = total + kept[h * HEAD_DIM : (h + 1) * HEAD_DIM]
    return total


def expand(compact, mask):
    size = compact.shape[1]
    tiled = jnp.concatenate([compact] * (size // HEAD_DIM), axis=0)
    return parts_of(jnp.where(mask, tiled, 0.0))


def kernel(cfg, q_hbm, k_hbm, v_hbm, g_hbm, w_hbm, mixed_ref, qg_ref, kg_ref, vg_ref, wg_ref,
           q_raw, k_raw, v_raw, g_raw, mixed_out, qg_out, kg_out, vg_out, wg_out, out_sem, halo, vpad, gpad, qf, kf, wpad, loc, vloc, kterm,
           attn_s, rden_s, dgw_s, state, stage, extra_s, w_raw, src_f, r1_f, tot_f, r2_f, res_f, r3_f,
           src_b, r1_b, tot_b, r2_b, res_b, r3_b,
           in_sem, halo_send, halo_recv, s1, v1, s2, v2, s3, v3):
    rows, cols, width, wide, nb, no, inner, per, first, fper = cfg
    group = nb * inner
    count = rows * COLS
    tm = lax.axis_index("tm")
    band = lax.axis_index("band")
    z = tm // inner
    tiles = wide // LANES
    a = tm % inner
    m = a * nb + band

    def peer_of(o):
        p = (m + o) % group
        return p, {"tm": z * inner + p // nb, "band": p % nb}

    def outer_of(o):
        zp = (z + o) % no
        return zp, {"tm": zp * inner + a, "band": band}

    loads = [
        [pltpu.make_async_copy(h.at[0, r], d.at[r], in_sem.at[i, r]) for r in range(rows)]
        for i, (h, d) in enumerate(((k_hbm, k_raw), (v_hbm, v_raw), (q_hbm, q_raw), (g_hbm, g_raw)))
    ]
    loads.append([pltpu.make_async_copy(w_hbm, w_raw, in_sem.at[4, 0])])
    for some in loads:
        for c in some:
            c.start()

    def loaded(i):
        for c in loads[i]:
            c.wait()

    halo[...] = jnp.zeros_like(halo)
    barrier = pltpu.get_barrier_semaphore()
    for o in range(1, group):
        pl.semaphore_signal(barrier, inc=1, device_id=peer_of(o)[1], device_id_type=MESH)
    for o in range(1, no):
        pl.semaphore_signal(barrier, inc=1, device_id=outer_of(o)[1], device_id_type=MESH)

    vpad[...] = jnp.zeros_like(vpad)
    gpad[...] = jnp.zeros_like(gpad)
    kf[...] = jnp.zeros_like(kf)
    kf[:, 0:cols, width:wide] = jnp.ones((rows, cols, wide - width), BF16)
    qf[...] = jnp.ones_like(qf)
    wpad[...] = jnp.zeros_like(wpad)
    src_f[...] = jnp.zeros_like(src_f)
    stage[...] = jnp.zeros_like(stage)

    def halo_copies(up):
        out = []
        for i, h in enumerate((v_hbm, g_hbm)):
            out.append(pltpu.make_async_remote_copy(
                src_ref=h.at[0, 0] if up else h.at[0, rows - 1],
                dst_ref=halo.at[i, 1 if up else 0],
                send_sem=halo_send.at[i, 1 if up else 0],
                recv_sem=halo_recv.at[i, 1 if up else 0],
                device_id={"band": band - 1 if up else band + 1},
                device_id_type=MESH,
            ))
        return out

    masks = {size: same_head(size) for _, size in groups(wide)}
    ones = {size: masks[size].astype(F32).astype(BF16) for size in masks}

    def spot(index):
        line = index % 16
        tile = index // 16
        return first + tile // per, line, (tile % per) * LANES

    def put(dst, at, size, compact, norm):
        for t in range(size // LANES):
            tile = at // LANES + t
            lane = (tile % per) * LANES
            for h in range(2):
                dst[2 * (tile // per) + h, :, lane : lane + LANES] = compact[
                    16 * h : 16 * h + 16, t * LANES : (t + 1) * LANES]
            slot, line, lane = spot(tile)
            dst[slot, line : line + 1, lane : lane + LANES] = norm[
                :, t * LANES : (t + 1) * LANES]

    def put_forward(at, size, compact, norm):
        for t in range(size // LANES):
            tile = at // LANES + t
            part = slice(t * LANES, (t + 1) * LANES)
            for h in range(4):
                slot, lane = (4 * tile + h) // fper, (4 * tile + h) % fper * LANES
                src_f[slot, :, lane : lane + LANES] = compact[8 * h : 8 * h + 8, part]
            piece = 4 * tiles + tile // 8
            slot, lane, line = piece // fper, piece % fper * LANES, tile % 8
            src_f[slot, line : line + 1, lane : lane + LANES] = norm[:, part]

    def norm_forward(at, size):
        lines = []
        for tile in range(at // LANES, (at + size) // LANES):
            piece = 4 * tiles + tile // 8
            slot, lane, line = piece // fper, piece % fper * LANES, tile % 8
            lines.append(r3_f[slot, line : line + 1, lane : lane + LANES])
        return jnp.concatenate(lines, axis=1) if len(lines) > 1 else lines[0]

    def phase1(way, src, r1):
        out = []
        for o in range(1, group):
            p, dev = peer_of(o)
            c = pltpu.make_async_remote_copy(
                src_ref=src.at[p], dst_ref=r1.at[m], send_sem=s1.at[way, o],
                recv_sem=v1.at[way, m], device_id=dev, device_id_type=MESH)
            c.start()
            out.append(c)
        r1[pl.ds(m, 1)] = src[pl.ds(m, 1)]
        return out

    def wait1(way, src, r1):
        for o in range(1, group):
            p, dev = peer_of(o)
            pltpu.make_async_remote_copy(
                src_ref=src.at[p], dst_ref=r1.at[p], send_sem=s1.at[way, o],
                recv_sem=v1.at[way, p], device_id=dev, device_id_type=MESH).wait_recv()

    def phase2(way, r1, tot, r2):
        total = r1[0].astype(F32)
        for j in range(1, group):
            total = total + r1[j].astype(F32)
        total = total.astype(tot.dtype)
        tot[...] = total
        out = []
        for o in range(1, no):
            zp, dev = outer_of(o)
            c = pltpu.make_async_remote_copy(
                src_ref=tot, dst_ref=r2.at[z], send_sem=s2.at[way, o],
                recv_sem=v2.at[way, z], device_id=dev, device_id_type=MESH)
            c.start()
            out.append(c)
        r2[pl.ds(z, 1)] = total[None]
        return out

    def wait2(way, tot, r2):
        for o in range(1, no):
            zp, dev = outer_of(o)
            pltpu.make_async_remote_copy(
                src_ref=tot, dst_ref=r2.at[zp], send_sem=s2.at[way, o],
                recv_sem=v2.at[way, zp], device_id=dev, device_id_type=MESH).wait_recv()

    def phase3(way, r1, r2, res, r3):
        backward = way == 1
        run = jnp.zeros(tot_f.shape if way == 0 else tot_b.shape, F32)
        whole = run
        for zz in range(no):
            part = r2[zz].astype(F32)
            earlier = (zz > z) if backward else (zz < z)
            run = run + jnp.where(earlier, part, 0.0)
            whole = whole + part
        if backward:
            line = lax.broadcasted_iota(jnp.int32, run.shape, 0)
            tile = lax.broadcasted_iota(jnp.int32, run.shape, 1) // LANES
            extra = ((m - first) * per + tile) * 16 + line >= tiles
        for aa in (range(inner - 1, -1, -1) if backward else range(inner)):
            for bb in range(nb):
                run = run + r1[aa * nb + bb].astype(F32)
            res[aa] = (jnp.where(extra, whole, run) if backward else run).astype(res.dtype)
        out = []
        for o in range(1, group):
            p, dev = peer_of(o)
            c = pltpu.make_async_remote_copy(
                src_ref=res.at[p // nb], dst_ref=r3.at[m], send_sem=s3.at[way, o],
                recv_sem=v3.at[way, m], device_id=dev, device_id_type=MESH)
            c.start()
            out.append(c)
        r3[pl.ds(m, 1)] = res[pl.ds(a, 1)]
        return out

    def wait3(way, res, r3):
        for o in range(1, group):
            p, dev = peer_of(o)
            pltpu.make_async_remote_copy(
                src_ref=res.at[p // nb], dst_ref=r3.at[p], send_sem=s3.at[way, o],
                recv_sem=v3.at[way, p], device_id=dev, device_id_type=MESH).wait_recv()
        if way == 0:
            for tile in range(tiles):
                for h in range(4):
                    slot, lane = (4 * tile + h) // fper, (4 * tile + h) % fper * LANES
                    state[8 * h : 8 * h + 8, tile * LANES : (tile + 1) * LANES] = r3[
                        slot, :, lane : lane + LANES]
            return
        for tile in range(tiles):
            lane = (tile % per) * LANES
            for h in range(2):
                state[16 * h : 16 * h + 16, tile * LANES : (tile + 1) * LANES] = r3[
                    2 * (tile // per) + h, :, lane : lane + LANES].astype(F32)
        extra_s[...] = r3[first:group].astype(F32)

    def norm_of(at, size):
        lines = []
        for t in range(at // LANES, (at + size) // LANES):
            slot, line, lane = spot(t)
            lines.append(extra_s[slot - first, line : line + 1, lane : lane + LANES])
        return jnp.concatenate(lines, axis=1) if len(lines) > 1 else lines[0]

    outs = ((mixed_out, mixed_ref), (qg_out, qg_ref), (kg_out, kg_ref), (vg_out, vg_ref))

    def writes(n):
        held, ref = outs[n]
        return [
            pltpu.make_async_copy(held.at[r], ref.at[0, r], out_sem.at[n, r]) for r in range(rows)
        ]

    def write(n):
        for c in writes(n):
            c.start()

    sent = []
    loaded(0)
    kf[:, 0:cols, 0:width] = feature(k_raw[...].astype(F32)).astype(BF16)
    loaded(1)
    vpad[1 : rows + 1, 0:cols, 0:width] = v_raw[...].astype(F32)
    for at, size in groups(wide):
        kg = kf[:, :, at : at + size].reshape(count, size)
        vg = vpad[1 : rows + 1, :, at : at + size].reshape(count, size).astype(BF16)
        own = compress(mm_at(kg, vg), masks[size])
        norm = jnp.sum(kg.astype(F32), axis=0, keepdims=True)
        put_forward(at, size, own, norm)
    pl.semaphore_wait(barrier, group - 1 + no - 1)
    sent += phase1(0, src_f, r1_f)

    @pl.when(band > 0)
    def _():
        for c in halo_copies(True):
            c.start()

    @pl.when(band < nb - 1)
    def _():
        for c in halo_copies(False):
            c.start()

    loaded(2)
    qf[:, 0:cols, 0:width] = feature(q_raw[...].astype(F32)).astype(BF16)
    loaded(3)
    gpad[1 : rows + 1, 0:cols, 0:width] = g_raw[...].astype(F32)
    loaded(4)
    for i in range(3):
        for j in range(3):
            wpad[3 * i + j : 3 * i + j + 1, 0:width] = w_raw[i, j : j + 1, :]

    def conv(t):
        lanes = pl.ds(pl.multiple_of(t * LANES, LANES), LANES)
        vb = vpad[:, :, lanes]
        gb = gpad[:, :, lanes]
        vs = (pltpu.roll(vb, 1, 1), vb, pltpu.roll(vb, COLS - 1, 1))
        gs = (pltpu.roll(gb, 1, 1), gb, pltpu.roll(gb, COLS - 1, 1))
        own = gb[1 : rows + 1]
        lo = jnp.zeros((rows, COLS, LANES), F32)
        vl = lo
        for i in range(3):
            for j in range(3):
                w = wpad[3 * i + j : 3 * i + j + 1, lanes].reshape(1, 1, LANES)
                near = vs[j][i : i + rows]
                lo = lo + w * near
                vl = vl + w * gs[2 - j][2 - i : 2 - i + rows]
                term = jnp.sum(jnp.sum(own * near, axis=0), axis=0, keepdims=True)
                kterm[3 * i + j : 3 * i + j + 1, lanes] = term
        loc[:, :, lanes] = lo
        vloc[:, :, lanes] = vl

    half = (tiles + 1) // 2
    wait1(0, src_f, r1_f)
    sent += phase2(0, r1_f, tot_f, r2_f)

    @pl.when(band > 0)
    def _():
        for c in halo_copies(False):
            c.wait_recv()

    @pl.when(band < nb - 1)
    def _():
        for c in halo_copies(True):
            c.wait_recv()

    for i, pad in enumerate((vpad, gpad)):
        pad[0, 0:cols, 0:width] = halo[i, 0].astype(F32)
        pad[rows + 1, 0:cols, 0:width] = halo[i, 1].astype(F32)
    pl.loop(0, half)(conv)
    wait2(0, tot_f, r2_f)
    sent += phase3(0, r1_f, r2_f, res_f, r3_f)
    pl.loop(half, tiles)(conv)
    for r in range(9):
        for t in range(tiles):
            slot, line, lane = spot(tiles * (r + 1) + t)
            stage[slot, line : line + 1, lane : lane + LANES] = kterm[
                r : r + 1, t * LANES : (t + 1) * LANES]
    wait3(0, res_f, r3_f)
    blocks = []
    for at, size in groups(wide):
        mask, one = masks[size], ones[size]
        high, low = expand(state[:, at : at + size], mask)
        norm = norm_forward(at, size)
        blocks.append((high, low, norm))
        qg = qf[:, :, at : at + size].reshape(count, size)
        gg = gpad[1 : rows + 1, :, at : at + size].reshape(count, size)
        dh, dl = parts_of(qg.astype(F32) * norm)
        den = mm(dh, one) + mm(dl, one)
        num = mm(qg, high) + mm(qg, low)
        rden = 1.0 / den
        attn = num * rden
        th, tl = parts_of(gg * attn)
        dgw = -(mm(th, one) + mm(tl, one)) * rden
        sh, sl = parts_of(gg * rden)
        own = compress(mm_at(qg, sh) + mm_at(qg, sl), mask)
        put(stage, at, size, own, jnp.sum(qg.astype(F32) * dgw, axis=0, keepdims=True))
        attn_s[:, at : at + size] = attn
        rden_s[:, at : at + size] = rden
        dgw_s[:, at : at + size] = dgw
    src_b[...] = stage[...].astype(BF16)
    sent += phase1(1, src_b, r1_b)
    mixed = (attn_s[...].reshape(rows, COLS, wide) + loc[...]).astype(BF16)
    mixed_out[...] = mixed[:, 0:cols, 0:width]
    write(0)
    wait1(1, src_b, r1_b)
    sent += phase2(1, r1_b, tot_b, r2_b)
    for (at, size), (high, low, norm) in zip(groups(wide), blocks):
        gg = gpad[1 : rows + 1, :, at : at + size].reshape(count, size)
        sh, sl = parts_of(gg * rden_s[:, at : at + size])
        back = mm_bt(sh, high) + mm_bt(sh, low) + mm_bt(sl, high)
        attn_s[:, at : at + size] = back + dgw_s[:, at : at + size] * norm
    grad = attn_s[...].reshape(rows, COLS, wide)[:, 0:cols, 0:width]
    qg_out[...] = (grad * slope(q_raw[...].astype(F32))).astype(BF16)
    write(1)
    wait2(1, tot_b, r2_b)
    sent += phase3(1, r1_b, r2_b, res_b, r3_b)
    steep = slope(k_raw[...].astype(F32))
    dgw_s[...] = jnp.ones_like(dgw_s)
    for r in range(rows):
        dgw_s[r * COLS : r * COLS + cols, 0:width] = steep[r]
    wait3(1, res_b, r3_b)
    for at, size in groups(wide):
        high, low = expand(state[:, at : at + size], masks[size])
        norm = norm_of(at, size)
        kg = kf[:, :, at : at + size].reshape(count, size)
        vg = vpad[1 : rows + 1, :, at : at + size].reshape(count, size).astype(BF16)
        back = mm_bt(vg, high) + mm_bt(vg, low) + norm
        attn_s[:, at : at + size] = back * dgw_s[:, at : at + size]
        rden_s[:, at : at + size] = mm(kg, high) + mm(kg, low) + vloc[
            :, :, at : at + size].reshape(count, size)
    for n, held, made in ((2, kg_out, attn_s), (3, vg_out, rden_s)):
        held[...] = made[...].reshape(rows, COLS, wide)[:, 0:cols, 0:width].astype(BF16)
        write(n)
    tokens = lax.axis_size("tm") * nb * rows * cols
    for r in range(9):
        for t in range(tiles):
            slot, line, lane = spot(tiles * (r + 1) + t)
            size = min(LANES, width - t * LANES)
            term = extra_s[slot - first, line : line + 1, lane : lane + size]
            wg_out[r // 3, r % 3 : r % 3 + 1, t * LANES : t * LANES + size] = term * (
                1.0 / math.sqrt(tokens))

    pltpu.make_async_copy(wg_out, wg_ref, out_sem.at[4, 0]).start()
    for n in range(4):
        for c in writes(n):
            c.wait()
    pltpu.make_async_copy(wg_out, wg_ref, out_sem.at[4, 0]).wait()
    for c in sent:
        c.wait_send()

    @pl.when(band > 0)
    def _():
        for c in halo_copies(True):
            c.wait_send()

    @pl.when(band < nb - 1)
    def _():
        for c in halo_copies(False):
            c.wait_send()


def shards(query_input, key_input, value_input, cotangent, local_kernel_weight):
    _, rows, cols, width = query_input.shape
    wide = -(-width // LANES) * LANES
    frames, nb = lax.axis_size("tm"), lax.axis_size("band")
    inner = 4
    no = frames // inner
    group = nb * inner
    tiles = wide // LANES
    per = -(-tiles // (group // 2))
    first = 2 * -(-tiles // per)
    lanes = per * LANES
    fper = -(-(4 * tiles + -(-tiles // 8)) // group)
    count = rows * COLS
    cfg = (rows, cols, width, wide, nb, no, inner, per, first, fper)
    raw = pltpu.VMEM((rows, cols, width), BF16)

    def buffers(r, lanes, kind):
        return [
            pltpu.VMEM((n, r, lanes) if n else (r, lanes), kind)
            for n in (group, group, 0, no, inner, group)
        ]

    tok = jax.ShapeDtypeStruct(query_input.shape, BF16)
    dma = pltpu.SemaphoreType.DMA
    made = pl.pallas_call(
        functools.partial(kernel, cfg),
        out_shape=(tok, tok, tok, tok, jax.ShapeDtypeStruct(local_kernel_weight.shape, F32)),
        in_specs=[pl.BlockSpec(memory_space=pltpu.HBM)] * 5,
        out_specs=[pl.BlockSpec(memory_space=pl.ANY)] * 5,
        scratch_shapes=[
            raw, raw, raw, raw, raw, raw, raw, raw,
            pltpu.VMEM(local_kernel_weight.shape, F32), dma((5, rows)),
            pltpu.VMEM((2, 2, cols, width), BF16),
            pltpu.VMEM((rows + 2, COLS, wide), F32), pltpu.VMEM((rows + 2, COLS, wide), F32),
            pltpu.VMEM((rows, COLS, wide), BF16), pltpu.VMEM((rows, COLS, wide), BF16),
            pltpu.VMEM((16, wide), F32),
            pltpu.VMEM((rows, COLS, wide), F32), pltpu.VMEM((rows, COLS, wide), F32),
            pltpu.VMEM((16, wide), F32),
            pltpu.VMEM((count, wide), F32), pltpu.VMEM((count, wide), F32),
            pltpu.VMEM((count, wide), F32),
            pltpu.VMEM((HEAD_DIM, wide), F32),
            pltpu.VMEM((group, 16, lanes), F32), pltpu.VMEM((group - first, 16, lanes), F32),
            pltpu.VMEM(local_kernel_weight.shape, F32),
            *buffers(8, fper * LANES, F32), *buffers(16, lanes, BF16),
            dma((5, rows)), dma((2, 2)), dma((2, 2)),
            dma((2, group)), dma((2, group)), dma((2, no)), dma((2, no)),
            dma((2, group)), dma((2, group)),
        ],
        compiler_params=pltpu.CompilerParams(
            collective_id=0, has_side_effects=True, vmem_limit_bytes=62 * 1024 * 1024
        ),
        cost_estimate=pl.CostEstimate(flops=10**9, bytes_accessed=3 * 10**6, transcendentals=0),
        name="block_causal",
    )(query_input, key_input, value_input, cotangent, local_kernel_weight)
    return pl.pallas_call(
        hand_over,
        out_shape=tuple(jax.ShapeDtypeStruct(x.shape, x.dtype) for x in made),
        in_specs=[pl.BlockSpec(memory_space=pl.ANY)] * 5,
        out_specs=[pl.BlockSpec(memory_space=pltpu.HBM)] * 5,
        scratch_shapes=[pltpu.VMEM(x.shape, x.dtype) for x in made]
        + [dma((5, rows)), dma((5, rows))],
        compiler_params=pltpu.CompilerParams(vmem_limit_bytes=62 * 1024 * 1024),
        name="hand_over",
    )(*made)


def hand_over(*refs):
    pieces = []
    for i in range(5):
        src, dst, held = refs[i], refs[5 + i], refs[10 + i]
        steps = range(src.shape[1]) if i < 4 else (None,)
        for r in steps:
            at = (lambda x, r=r: x if r is None else x.at[0, r])
            n = 0 if r is None else r
            pieces.append((
                pltpu.make_async_copy(at(src), at(held), refs[15].at[i, n]),
                pltpu.make_async_copy(at(held), at(dst), refs[16].at[i, n]),
            ))
    for load, _ in pieces:
        load.start()
    for load, store in pieces:
        load.wait()
        store.start()
    for _, store in pieces:
        store.wait()


def solution(mesh):
    token = P("tm", "band", None, None)
    return jax.shard_map(
        shards,
        mesh=mesh,
        in_specs=(token,) * 4 + (P(),),
        out_specs=(token,) * 4 + (P(),),
        check_vma=False,
    )
```

profile of v0, /device:TPU:0, one launch (start us, length us, event | category | flops | bytes accessed | tf_op | source)
XLA Modules:
  0.0 35.3 jit_solution(12401455993423956872)
XLA Ops:
  0.6 32.1 %block_causal.1 = (bf16[1,5,26,1120]{3,2,1,0:T(8,128)(2,1)}, bf16[1,5,26,1120]{3,2,1,0:T(8,128)(2,1)}, bf16[1,5,26,1120]{3,2,1,0:T(8,128)(2,1)}, bf16[1,5,26,1120]{3,2,1,0:T(8,128)(2,1)}, f32[3,3,1120]{2,1,0:T(4,128)}) custom-call(bf16[1,5,26,1120]{3,2,1,0:T(8,128)(2,1)} %q_hbm.1, bf16[1,5,26,1120]{3,2,1,0:T(8,128)(2,1)} %k_hbm.1, ...), custom_call_target="tpu_custom_call" | custom-call | flops 1000000000 | bytes 3000000 | tf_op jit(solution)/shard_map/block_causal/pallas_call | solution.py:474
  32.8 2.5 %hand_over.1 = (bf16[1,5,26,1120]{3,2,1,0:T(8,128)(2,1)}, bf16[1,5,26,1120]{3,2,1,0:T(8,128)(2,1)}, bf16[1,5,26,1120]{3,2,1,0:T(8,128)(2,1)}, bf16[1,5,26,1120]{3,2,1,0:T(8,128)(2,1)}, f32[3,3,1120]{2,1,0:T(4,128)}) custom-call(bf16[1,5,26,1120]{3,2,1,0:T(8,128)(2,1)} %get-tuple-element.10.refs_0_, bf16[1,5,26,1120]{3,2,1,0:T(8,128)(2,1)} %get-tuple-element.11.refs_1_, ...), custom_call_target="tpu_custom_call" | custom-call | tf_op jit(solution)/shard_map/hand_over/pallas_call | solution.py:504
where the time goes:
time: 35.6 us; the launch traced here: 35.3 us
  Pallas kernels  34.7 us (97%)
  between operations  0.64 us (2%)
    pallas_call x1, Pallas kernels, shards(): pl.pallas_call(functools.partial(kernel, cfg), out_shape=(tok, tok, tok,...  32.1 us
    pallas_call x1, Pallas kernels, shards(): pl.pallas_call(hand_over, out_shape=tuple((jax.ShapeDtypeStruct(x.shape,...  2.53 us

commit v1 on v0

--- a/solution.py
+++ b/solution.py
@@ -407,18 +407,25 @@
     for r in range(rows):
         dgw_s[r * COLS : r * COLS + cols, 0:width] = steep[r]
     wait3(1, res_b, r3_b)
+
+    def send_out(n, held, made):
+        held[...] = made[...].reshape(rows, COLS, wide)[:, 0:cols, 0:width].astype(BF16)
+        write(n)
+
+    later = []
     for at, size in groups(wide):
         high, low = expand(state[:, at : at + size], masks[size])
         norm = norm_of(at, size)
-        kg = kf[:, :, at : at + size].reshape(count, size)
+        later.append((high, low))
         vg = vpad[1 : rows + 1, :, at : at + size].reshape(count, size).astype(BF16)
         back = mm_bt(vg, high) + mm_bt(vg, low) + norm
         attn_s[:, at : at + size] = back * dgw_s[:, at : at + size]
+    send_out(2, kg_out, attn_s)
+    for (at, size), (high, low) in zip(groups(wide), later):
+        kg = kf[:, :, at : at + size].reshape(count, size)
         rden_s[:, at : at + size] = mm(kg, high) + mm(kg, low) + vloc[
             :, :, at : at + size].reshape(count, size)
-    for n, held, made in ((2, kg_out, attn_s), (3, vg_out, rden_s)):
-        held[...] = made[...].reshape(rows, COLS, wide)[:, 0:cols, 0:width].astype(BF16)
-        write(n)
+    send_out(3, vg_out, rden_s)
     tokens = lax.axis_size("tm") * nb * rows * cols
     for r in range(9):
         for t in range(tiles):
@@ -507,7 +514,7 @@
         in_specs=[pl.BlockSpec(memory_space=pl.ANY)] * 5,
         out_specs=[pl.BlockSpec(memory_space=pltpu.HBM)] * 5,
         scratch_shapes=[pltpu.VMEM(x.shape, x.dtype) for x in made]
-        + [dma((5, rows)), dma((5, rows))],
+        + [dma((5,)), dma((5,))],
         compiler_params=pltpu.CompilerParams(vmem_limit_bytes=62 * 1024 * 1024),
         name="hand_over",
     )(*made)
@@ -517,14 +524,10 @@
     pieces = []
     for i in range(5):
         src, dst, held = refs[i], refs[5 + i], refs[10 + i]
-        steps = range(src.shape[1]) if i < 4 else (None,)
-        for r in steps:
-            at = (lambda x, r=r: x if r is None else x.at[0, r])
-            n = 0 if r is None else r
-            pieces.append((
-                pltpu.make_async_copy(at(src), at(held), refs[15].at[i, n]),
-                pltpu.make_async_copy(at(held), at(dst), refs[16].at[i, n]),
-            ))
+        pieces.append((
+            pltpu.make_async_copy(src, held, refs[15].at[i]),
+            pltpu.make_async_copy(held, dst, refs[16].at[i]),
+        ))
     for load, _ in pieces:
         load.start()
     for load, store in pieces:

time: 35.6 us -> 35.1 us (0.986)
  Pallas kernels: 34.7 us -> 34.2 us
where the time goes in v1:
time: 35.1 us; the launch traced here: 34.9 us
  Pallas kernels  34.2 us (97%)
  between operations  0.64 us (2%)
    pallas_call x1, Pallas kernels, shards(): pl.pallas_call(functools.partial(kernel, cfg), out_shape=(tok, tok, tok,...  32 us
    pallas_call x1, Pallas kernels, shards(): pl.pallas_call(hand_over, out_shape=tuple((jax.ShapeDtypeStruct(x.shape,...  2.18 us

profile of v1, /device:TPU:0, one launch (start us, length us, event | category | flops | bytes accessed | tf_op | source)
XLA Modules:
  0.0 34.9 jit_solution(16137904774761381039)
XLA Ops:
  0.6 32.0 %block_causal.1 = (bf16[1,5,26,1120]{3,2,1,0:T(8,128)(2,1)}, bf16[1,5,26,1120]{3,2,1,0:T(8,128)(2,1)}, bf16[1,5,26,1120]{3,2,1,0:T(8,128)(2,1)}, bf16[1,5,26,1120]{3,2,1,0:T(8,128)(2,1)}, f32[3,3,1120]{2,1,0:T(4,128)}) custom-call(bf16[1,5,26,1120]{3,2,1,0:T(8,128)(2,1)} %q_hbm.1, bf16[1,5,26,1120]{3,2,1,0:T(8,128)(2,1)} %k_hbm.1, ...), custom_call_target="tpu_custom_call" | custom-call | flops 1000000000 | bytes 3000000 | tf_op jit(solution)/shard_map/block_causal/pallas_call | solution.py:481
  32.7 2.2 %hand_over.1 = (bf16[1,5,26,1120]{3,2,1,0:T(8,128)(2,1)}, bf16[1,5,26,1120]{3,2,1,0:T(8,128)(2,1)}, bf16[1,5,26,1120]{3,2,1,0:T(8,128)(2,1)}, bf16[1,5,26,1120]{3,2,1,0:T(8,128)(2,1)}, f32[3,3,1120]{2,1,0:T(4,128)}) custom-call(bf16[1,5,26,1120]{3,2,1,0:T(8,128)(2,1)} %get-tuple-element.10.refs_0_, bf16[1,5,26,1120]{3,2,1,0:T(8,128)(2,1)} %get-tuple-element.11.refs_1_, ...), custom_call_target="tpu_custom_call" | custom-call | tf_op jit(solution)/shard_map/hand_over/pallas_call | solution.py:511

commit v2 on v1

--- a/solution.py
+++ b/solution.py
@@ -86,26 +86,29 @@
     a = tm % inner
     m = a * nb + band
 
+    def placed(p):
+        frame = lax.div(p, nb)
+        return p, frame, {"tm": z * inner + frame, "band": lax.rem(p, nb)}
+
+    peers = [None] + [placed(lax.rem(m + o, group)) for o in range(1, group)]
+    outers = [lax.rem(z + o, no) for o in range(no)]
+
     def peer_of(o):
-        p = (m + o) % group
-        return p, {"tm": z * inner + p // nb, "band": p % nb}
+        return peers[o][0], peers[o][2]
 
     def outer_of(o):
-        zp = (z + o) % no
-        return zp, {"tm": zp * inner + a, "band": band}
+        return outers[o], {"tm": outers[o] * inner + a, "band": band}
 
     loads = [
-        [pltpu.make_async_copy(h.at[0, r], d.at[r], in_sem.at[i, r]) for r in range(rows)]
+        pltpu.make_async_copy(h.at[0], d, in_sem.at[i])
         for i, (h, d) in enumerate(((k_hbm, k_raw), (v_hbm, v_raw), (q_hbm, q_raw), (g_hbm, g_raw)))
     ]
-    loads.append([pltpu.make_async_copy(w_hbm, w_raw, in_sem.at[4, 0])])
-    for some in loads:
-        for c in some:
-            c.start()
+    loads.append(pltpu.make_async_copy(w_hbm, w_raw, in_sem.at[4]))
+    for c in loads[:2]:
+        c.start()
 
     def loaded(i):
-        for c in loads[i]:
-            c.wait()
+        loads[i].wait()
 
     halo[...] = jnp.zeros_like(halo)
     barrier = pltpu.get_barrier_semaphore()
@@ -114,6 +117,8 @@
     for o in range(1, no):
         pl.semaphore_signal(barrier, inc=1, device_id=outer_of(o)[1], device_id_type=MESH)
 
+    for c in loads[2:]:
+        c.start()
     vpad[...] = jnp.zeros_like(vpad)
     gpad[...] = jnp.zeros_like(gpad)
     kf[...] = jnp.zeros_like(kf)
@@ -238,7 +243,7 @@
         for o in range(1, group):
             p, dev = peer_of(o)
             c = pltpu.make_async_remote_copy(
-                src_ref=res.at[p // nb], dst_ref=r3.at[m], send_sem=s3.at[way, o],
+                src_ref=res.at[peers[o][1]], dst_ref=r3.at[m], send_sem=s3.at[way, o],
                 recv_sem=v3.at[way, m], device_id=dev, device_id_type=MESH)
             c.start()
             out.append(c)
@@ -249,7 +254,7 @@
         for o in range(1, group):
             p, dev = peer_of(o)
             pltpu.make_async_remote_copy(
-                src_ref=res.at[p // nb], dst_ref=r3.at[p], send_sem=s3.at[way, o],
+                src_ref=res.at[peers[o][1]], dst_ref=r3.at[p], send_sem=s3.at[way, o],
                 recv_sem=v3.at[way, p], device_id=dev, device_id_type=MESH).wait_recv()
         if way == 0:
             for tile in range(tiles):
@@ -276,13 +281,10 @@
 
     def writes(n):
         held, ref = outs[n]
-        return [
-            pltpu.make_async_copy(held.at[r], ref.at[0, r], out_sem.at[n, r]) for r in range(rows)
-        ]
+        return pltpu.make_async_copy(held, ref.at[0], out_sem.at[n])
 
     def write(n):
-        for c in writes(n):
-            c.start()
+        writes(n).start()
 
     sent = []
     loaded(0)
@@ -402,6 +404,19 @@
     write(1)
     wait2(1, tot_b, r2_b)
     sent += phase3(1, r1_b, r2_b, res_b, r3_b)
+    for c in sent[: -(group - 1)]:
+        c.wait_send()
+
+    @pl.when(band > 0)
+    def _():
+        for c in halo_copies(True):
+            c.wait_send()
+
+    @pl.when(band < nb - 1)
+    def _():
+        for c in halo_copies(False):
+            c.wait_send()
+
     steep = slope(k_raw[...].astype(F32))
     dgw_s[...] = jnp.ones_like(dgw_s)
     for r in range(rows):
@@ -435,23 +450,12 @@
             wg_out[r // 3, r % 3 : r % 3 + 1, t * LANES : t * LANES + size] = term * (
                 1.0 / math.sqrt(tokens))
 
-    pltpu.make_async_copy(wg_out, wg_ref, out_sem.at[4, 0]).start()
+    pltpu.make_async_copy(wg_out, wg_ref, out_sem.at[4]).start()
     for n in range(4):
-        for c in writes(n):
-            c.wait()
-    pltpu.make_async_copy(wg_out, wg_ref, out_sem.at[4, 0]).wait()
-    for c in sent:
+        writes(n).wait()
+    pltpu.make_async_copy(wg_out, wg_ref, out_sem.at[4]).wait()
+    for c in sent[-(group - 1) :]:
         c.wait_send()
-
-    @pl.when(band > 0)
-    def _():
-        for c in halo_copies(True):
-            c.wait_send()
-
-    @pl.when(band < nb - 1)
-    def _():
-        for c in halo_copies(False):
-            c.wait_send()
 
 
 def shards(query_input, key_input, value_input, cotangent, local_kernel_weight):
@@ -485,7 +489,7 @@
         out_specs=[pl.BlockSpec(memory_space=pl.ANY)] * 5,
         scratch_shapes=[
             raw, raw, raw, raw, raw, raw, raw, raw,
-            pltpu.VMEM(local_kernel_weight.shape, F32), dma((5, rows)),
+            pltpu.VMEM(local_kernel_weight.shape, F32), dma((5,)),
             pltpu.VMEM((2, 2, cols, width), BF16),
             pltpu.VMEM((rows + 2, COLS, wide), F32), pltpu.VMEM((rows + 2, COLS, wide), F32),
             pltpu.VMEM((rows, COLS, wide), BF16), pltpu.VMEM((rows, COLS, wide), BF16),
@@ -498,7 +502,7 @@
             pltpu.VMEM((group, 16, lanes), F32), pltpu.VMEM((group - first, 16, lanes), F32),
             pltpu.VMEM(local_kernel_weight.shape, F32),
             *buffers(8, fper * LANES, F32), *buffers(16, lanes, BF16),
-            dma((5, rows)), dma((2, 2)), dma((2, 2)),
+            dma((5,)), dma((2, 2)), dma((2, 2)),
             dma((2, group)), dma((2, group)), dma((2, no)), dma((2, no)),
             dma((2, group)), dma((2, group)),
         ],

time: 35.1 us -> 34.6 us (0.986)
  Pallas kernels: 34.2 us -> 33.8 us
    pallas_call x1, Pallas kernels: 32 us -> 31.6 us  [shards(): pl.pallas_call(functools.partial(kernel, cfg), out_shape=(tok, tok, tok,...]
where the time goes in v2:
time: 34.6 us; the launch traced here: 34.4 us
  Pallas kernels  33.8 us (98%)
  between operations  0.64 us (2%)
    pallas_call x1, Pallas kernels, shards(): pl.pallas_call(functools.partial(kernel, cfg), out_shape=(tok, tok, tok,...  31.6 us
    pallas_call x1, Pallas kernels, shards(): pl.pallas_call(hand_over, out_shape=tuple((jax.ShapeDtypeStruct(x.shape,...  2.18 us

profile of v2, /device:TPU:0, one launch (start us, length us, event | category | flops | bytes accessed | tf_op | source)
XLA Modules:
  0.0 34.4 jit_solution(1423272180715819632)
XLA Ops:
  0.6 31.6 %block_causal.1 = (bf16[1,5,26,1120]{3,2,1,0:T(8,128)(2,1)}, bf16[1,5,26,1120]{3,2,1,0:T(8,128)(2,1)}, bf16[1,5,26,1120]{3,2,1,0:T(8,128)(2,1)}, bf16[1,5,26,1120]{3,2,1,0:T(8,128)(2,1)}, f32[3,3,1120]{2,1,0:T(4,128)}) custom-call(bf16[1,5,26,1120]{3,2,1,0:T(8,128)(2,1)} %q_hbm.1, bf16[1,5,26,1120]{3,2,1,0:T(8,128)(2,1)} %k_hbm.1, ...), custom_call_target="tpu_custom_call" | custom-call | flops 1000000000 | bytes 3000000 | tf_op jit(solution)/shard_map/block_causal/pallas_call | solution.py:485
  32.2 2.2 %hand_over.1 = (bf16[1,5,26,1120]{3,2,1,0:T(8,128)(2,1)}, bf16[1,5,26,1120]{3,2,1,0:T(8,128)(2,1)}, bf16[1,5,26,1120]{3,2,1,0:T(8,128)(2,1)}, bf16[1,5,26,1120]{3,2,1,0:T(8,128)(2,1)}, f32[3,3,1120]{2,1,0:T(4,128)}) custom-call(bf16[1,5,26,1120]{3,2,1,0:T(8,128)(2,1)} %get-tuple-element.10.refs_0_, bf16[1,5,26,1120]{3,2,1,0:T(8,128)(2,1)} %get-tuple-element.11.refs_1_, ...), custom_call_target="tpu_custom_call" | custom-call | tf_op jit(solution)/shard_map/hand_over/pallas_call | solution.py:515

commit v3 on v2

--- a/solution.py
+++ b/solution.py
@@ -381,8 +381,8 @@
         attn = num * rden
         th, tl = parts_of(gg * attn)
         dgw = -(mm(th, one) + mm(tl, one)) * rden
-        sh, sl = parts_of(gg * rden)
-        own = compress(mm_at(qg, sh) + mm_at(qg, sl), mask)
+        sh = (gg * rden).astype(BF16)
+        own = compress(mm_at(qg, sh), mask)
         put(stage, at, size, own, jnp.sum(qg.astype(F32) * dgw, axis=0, keepdims=True))
         attn_s[:, at : at + size] = attn
         rden_s[:, at : at + size] = rden
@@ -429,16 +429,16 @@
 
     later = []
     for at, size in groups(wide):
-        high, low = expand(state[:, at : at + size], masks[size])
+        high = expand(state[:, at : at + size], masks[size])[0]
         norm = norm_of(at, size)
-        later.append((high, low))
+        later.append(high)
         vg = vpad[1 : rows + 1, :, at : at + size].reshape(count, size).astype(BF16)
-        back = mm_bt(vg, high) + mm_bt(vg, low) + norm
+        back = mm_bt(vg, high) + norm
         attn_s[:, at : at + size] = back * dgw_s[:, at : at + size]
     send_out(2, kg_out, attn_s)
-    for (at, size), (high, low) in zip(groups(wide), later):
+    for (at, size), high in zip(groups(wide), later):
         kg = kf[:, :, at : at + size].reshape(count, size)
-        rden_s[:, at : at + size] = mm(kg, high) + mm(kg, low) + vloc[
+        rden_s[:, at : at + size] = mm(kg, high) + vloc[
             :, :, at : at + size].reshape(count, size)
     send_out(3, vg_out, rden_s)
     tokens = lax.axis_size("tm") * nb * rows * cols

time: 34.6 us -> 34.1 us (0.986)
  Pallas kernels: 33.8 us -> 33.3 us
    pallas_call x1, Pallas kernels: 31.6 us -> 31.1 us  [shards(): pl.pallas_call(functools.partial(kernel, cfg), out_shape=(tok, tok, tok,...]
where the time goes in v3:
time: 34.1 us; the launch traced here: 33.9 us
  Pallas kernels  33.3 us (98%)
  between operations  0.64 us (2%)
    pallas_call x1, Pallas kernels, shards(): pl.pallas_call(functools.partial(kernel, cfg), out_shape=(tok, tok, tok,...  31.1 us
    pallas_call x1, Pallas kernels, shards(): pl.pallas_call(hand_over, out_shape=tuple((jax.ShapeDtypeStruct(x.shape,...  2.18 us

profile of v3, /device:TPU:0, one launch (start us, length us, event | category | flops | bytes accessed | tf_op | source)
XLA Modules:
  0.0 33.9 jit_solution(9665279713388817137)
XLA Ops:
  0.6 31.1 %block_causal.1 = (bf16[1,5,26,1120]{3,2,1,0:T(8,128)(2,1)}, bf16[1,5,26,1120]{3,2,1,0:T(8,128)(2,1)}, bf16[1,5,26,1120]{3,2,1,0:T(8,128)(2,1)}, bf16[1,5,26,1120]{3,2,1,0:T(8,128)(2,1)}, f32[3,3,1120]{2,1,0:T(4,128)}) custom-call(bf16[1,5,26,1120]{3,2,1,0:T(8,128)(2,1)} %q_hbm.1, bf16[1,5,26,1120]{3,2,1,0:T(8,128)(2,1)} %k_hbm.1, ...), custom_call_target="tpu_custom_call" | custom-call | flops 1000000000 | bytes 3000000 | tf_op jit(solution)/shard_map/block_causal/pallas_call | solution.py:485
  31.7 2.2 %hand_over.1 = (bf16[1,5,26,1120]{3,2,1,0:T(8,128)(2,1)}, bf16[1,5,26,1120]{3,2,1,0:T(8,128)(2,1)}, bf16[1,5,26,1120]{3,2,1,0:T(8,128)(2,1)}, bf16[1,5,26,1120]{3,2,1,0:T(8,128)(2,1)}, f32[3,3,1120]{2,1,0:T(4,128)}) custom-call(bf16[1,5,26,1120]{3,2,1,0:T(8,128)(2,1)} %get-tuple-element.10.refs_0_, bf16[1,5,26,1120]{3,2,1,0:T(8,128)(2,1)} %get-tuple-element.11.refs_1_, ...), custom_call_target="tpu_custom_call" | custom-call | tf_op jit(solution)/shard_map/hand_over/pallas_call | solution.py:515

commit v4 on v3

--- a/solution.py
+++ b/solution.py
@@ -181,7 +181,7 @@
 
     def phase1(way, src, r1):
         out = []
-        for o in range(1, group):
+        for o in sorted(range(1, group), key=lambda n: -min(n, group - n)):
             p, dev = peer_of(o)
             c = pltpu.make_async_remote_copy(
                 src_ref=src.at[p], dst_ref=r1.at[m], send_sem=s1.at[way, o],
@@ -240,7 +240,7 @@
                 run = run + r1[aa * nb + bb].astype(F32)
             res[aa] = (jnp.where(extra, whole, run) if backward else run).astype(res.dtype)
         out = []
-        for o in range(1, group):
+        for o in sorted(range(1, group), key=lambda n: -min(n, group - n)):
             p, dev = peer_of(o)
             c = pltpu.make_async_remote_copy(
                 src_ref=res.at[peers[o][1]], dst_ref=r3.at[m], send_sem=s3.at[way, o],

time: 34.1 us -> 34 us (level)
  no operation moved by 1% of the time
where the time goes in v4:
time: 34 us; the launch traced here: 33.9 us
  Pallas kernels  33.2 us (98%)
  between operations  0.64 us (2%)
    pallas_call x1, Pallas kernels, shards(): pl.pallas_call(functools.partial(kernel, cfg), out_shape=(tok, tok, tok,...  31.1 us
    pallas_call x1, Pallas kernels, shards(): pl.pallas_call(hand_over, out_shape=tuple((jax.ShapeDtypeStruct(x.shape,...  2.18 us

profile of v4, /device:TPU:0, one launch (start us, length us, event | category | flops | bytes accessed | tf_op | source)
XLA Modules:
  0.0 33.9 jit_solution(8416683375509437240)
XLA Ops:
  0.6 31.1 %block_causal.1 = (bf16[1,5,26,1120]{3,2,1,0:T(8,128)(2,1)}, bf16[1,5,26,1120]{3,2,1,0:T(8,128)(2,1)}, bf16[1,5,26,1120]{3,2,1,0:T(8,128)(2,1)}, bf16[1,5,26,1120]{3,2,1,0:T(8,128)(2,1)}, f32[3,3,1120]{2,1,0:T(4,128)}) custom-call(bf16[1,5,26,1120]{3,2,1,0:T(8,128)(2,1)} %q_hbm.1, bf16[1,5,26,1120]{3,2,1,0:T(8,128)(2,1)} %k_hbm.1, ...), custom_call_target="tpu_custom_call" | custom-call | flops 1000000000 | bytes 3000000 | tf_op jit(solution)/shard_map/block_causal/pallas_call | solution.py:485
  31.7 2.2 %hand_over.1 = (bf16[1,5,26,1120]{3,2,1,0:T(8,128)(2,1)}, bf16[1,5,26,1120]{3,2,1,0:T(8,128)(2,1)}, bf16[1,5,26,1120]{3,2,1,0:T(8,128)(2,1)}, bf16[1,5,26,1120]{3,2,1,0:T(8,128)(2,1)}, f32[3,3,1120]{2,1,0:T(4,128)}) custom-call(bf16[1,5,26,1120]{3,2,1,0:T(8,128)(2,1)} %get-tuple-element.10.refs_0_, bf16[1,5,26,1120]{3,2,1,0:T(8,128)(2,1)} %get-tuple-element.11.refs_1_, ...), custom_call_target="tpu_custom_call" | custom-call | tf_op jit(solution)/shard_map/hand_over/pallas_call | solution.py:515
